TPU v7x, 256 devices: a whole 4x4x8 slice. The times are simulated.
256 devices in a mesh: rep: 32 (over z, x_hi, core), exp: 8 (over x_lo, y).
Axes of the slice: x: 4 (x_hi: 2, x_lo: 2; x = x_hi * 2 + x_lo), y: 4, z: 8, core: 2. Of those that a mesh axis runs over, the one named last changes fastest.
Arguments:
- tokens: bfloat16 [24576, 7168], P('rep'), may hold values from -6 to 6
- gates: float32 [24576, 8], P('rep'), may hold values from 0.1 to 1
- assign: int32 [24576, 8], P('rep'), may hold values from 0 to 7, each once within a row
- master: float32 [8, 224, 128, 256], P('exp', 'rep')
- owner: int32 [8, 224], P('exp'), may hold values from 0 to 31, as said below
Outputs:
- combined: bfloat16 [24576, 1024], P(('rep', 'exp'))
Inputs may be any that keep to these rules, and one draw needn't show every extreme that they name: `owner`: in each row, every index of rep owns exactly 7 buckets.
All inputs are finite; a program needn't handle non-finite values.
Results may differ from a plain program's by a relative error of at most 0.001.
Values may be sent and summed in bfloat16 or wider, within the bound.
A program may use at most 192 MiB of HBM per device.

v0:
```python
import jax
import jax.numpy as jnp
from jax import lax
from jax.sharding import PartitionSpec as P

D = 7168
FW = 1024
BLK = 128


QUANT_LIMIT = 448.0
GRID_STEP = 16.0


def nearest_even(scaled):
    shifted = scaled / GRID_STEP + 0.5
    level = jnp.floor(shifted)
    halfway = shifted == level
    odd_level = level - 2.0 * jnp.floor(level * 0.5) == 1.0
    level = jnp.where(jnp.logical_and(halfway, odd_level), level - 1.0, level)
    return level * GRID_STEP


def serve_tiles(master_slots):
    slot_count = master_slots.shape[0]
    blocks_view = master_slots.reshape(slot_count, BLK, 2, BLK)
    block_peak = jnp.max(jnp.abs(blocks_view), axis=(1, 3))
    block_scale = jnp.full_like(block_peak, 2.0 ** (-30))
    reciprocal = jnp.full_like(block_peak, 2.0**30)
    for exponent in range(-30, 1):
        exceeds = block_peak > QUANT_LIMIT * 2.0**exponent
        block_scale = jnp.where(exceeds, 2.0 ** (exponent + 1), block_scale)
        reciprocal = jnp.where(exceeds, 2.0 ** (-exponent - 1), reciprocal)
    scaled = blocks_view * reciprocal[:, None, :, None]
    quantized = nearest_even(scaled)
    served_tile = (quantized * block_scale[:, None, :, None]).astype(jnp.bfloat16)
    return jnp.transpose(served_tile, (0, 2, 3, 1)).reshape(slot_count, 2 * BLK, BLK)


def place_all(served_tiles, slot_bucket):
    inverse = jnp.argsort(slot_bucket)
    return jnp.take(served_tiles, inverse, axis=0)


def on_device(tokens, gates, assign, master, owner):
    master_slots = master[0]
    slot_bucket = jnp.argsort(owner[0], stable=True)
    tok_count = tokens.shape[0]
    split_rows = tokens.reshape(tok_count, D // BLK, BLK)
    exp_index = lax.axis_index("exp")
    gate_pick = jnp.sum(jnp.where(assign == exp_index, gates, jnp.zeros_like(gates)), axis=1)
    rows_here = tok_count // lax.axis_size("exp")
    served_tiles = lax.all_gather(serve_tiles(master_slots), "rep", axis=0, tiled=True)
    bucket_tiles = place_all(served_tiles, slot_bucket)
    placed = bucket_tiles.reshape(D // BLK, FW // (2 * BLK), 2 * BLK, BLK)
    projection = jnp.einsum("trk,rcfk->tcf", split_rows, placed, preferred_element_type=jnp.float32)
    combined = lax.psum_scatter(
        gate_pick[:, None] * projection.reshape(lax.axis_size("exp") * rows_here, FW),
        "exp",
        scatter_dimension=0,
        tiled=True,
    )
    return combined.astype(jnp.bfloat16)


def solution(mesh):
    return jax.shard_map(
        on_device,
        mesh=mesh,
        in_specs=(
            P("rep", None),
            P("rep", None),
            P("rep", None),
            P("exp", "rep", None, None),
            P("exp", None),
        ),
        out_specs=P(("rep", "exp"), None),
        check_vma=False,
    )
```

profile of v0, /device:TPU:8, one launch (start us, length us, event | category | flops | bytes accessed | tf_op | source)
XLA Modules:
  0.0 231.8 jit_solution(1880630947694374944)
XLA Ops:
  6.5 0.0 all-gather.2.cloned.1.call-start
  6.5 1.2 abs_reduce_fusion
  7.8 1.5 copy.21
  9.3 0.1 reduce_max.18
  9.5 1.3 fusion.9
  10.8 0.0 all-gather.2.cloned.1.call-update
  10.8 0.0 reduce-scatter.2.cloned.1.call-start
  10.8 3.8 %sort.34 = (s32[224]{0:T(256)}, s32[224]{0:T(256)S(1)}) sort(s32[224]{0:T(256)} %bitcast.21, s32[224]{0:T(256)S(1)} %iota.8), dimensions={0}, to_apply=%region_1.2 | sort | flops 1792 | bytes 3584 | tf_op jit(solution)/shard_map/jit(argsort)/sort | solution.py:47
  14.7 3.2 %sort.35 = (s32[224]{0:T(256)}, s32[224]{0:T(256)S(1)}) sort(s32[224]{0:T(256)S(1)} %get-tuple-element.7, s32[224]{0:T(256)S(1)} %iota.9), dimensions={0}, to_apply=%region_2.3 | sort | flops 1792 | bytes 3584 | tf_op jit(solution)/shard_map/jit(argsort)/sort | solution.py:41
  17.9 0.1 broadcast_in_dim.202
  18.0 0.0 copy-start
  18.0 0.0 copy-start.1
  18.0 10.5 %copy.24 = bf16[96,8,56,128]{3,2,1,0:T(8,128)(2,1)} copy(bf16[96,8,56,128]{3,1,2,0:T(8,128)(2,1)} %bitcast.16) | data formatting | bytes 22020096
  28.5 0.0 copy-done
  28.5 0.0 copy-done.1
  28.6 112.6 %all-gather.2.cloned.1.call-done = bf16[224,256,128]{2,1,0:T(8,128)(2,1)} async-done(((bf16[7,256,128]{2,1,0:T(8,128)(2,1)}), bf16[224,256,128]{2,1,0:T(8,128)(2,1)}) %all-gather.2.cloned.1.call-update) | async-done | bytes 14680080 | tf_op jit(solution)/shard_map/all_gather | solution.py:53
  141.2 14.4 %gather_fusion = bf16[224,256,128]{2,1,0:T(8,128)(2,1)} fusion(bf16[224,256,128]{2,1,0:T(8,128)(2,1)} %all-gather.2.cloned.1.call-done, s32[1024]{0:T(1024)S(1)} %pad_clamp_fusion), kind=kCustom, calls=%fused_computation | custom fusion | bytes 29361024 | tf_op jit(solution)/shard_map/jit(_take)/gather | solution.py:42
  155.6 19.2 %fusion = f32[4,256,768,1]{2,1,0,3:T(8,128)} fusion(bf16[56,4,256,128]{3,2,1,0:T(8,128)(2,1)} %bitcast.15, pred[56,4]{1,0:T(8,128)(4,1)S(1)} %broadcast_in_dim.202, bf16[768,56,128,1]{2,1,0,3:T(8,128)(2,1)} %bitcast.17), kind=kOutput, calls=%fused_computation.1 | convolution fusion | flops 11281629184 | bytes 28836064 | tf_op jit(solution)/shard_map/trk,rcfk->tcf/dot_general | solution.py:56
  174.8 2.4 %copy.19 = f32[768,1024]{1,0:T(8,128)S(1)} copy(f32[768,1024]{0,1:T(8,128)} %bitcast.19) | data formatting | bytes 6291456 | tf_op jit(solution)/shard_map/reshape | solution.py:58
  177.2 1.9 broadcast_multiply_fusion
  179.1 0.0 reduce-scatter.2.cloned.1.call-update
  179.1 44.2 %reduce-scatter.2.cloned.1.call-done = f32[96,1024]{1,0:T(8,128)} async-done(((f32[768,1024]{1,0:T(8,128)}), f32[96,1024]{1,0:T(8,128)}) %reduce-scatter.2.cloned.1.call-update) | async-done | bytes 393232 | tf_op jit(solution)/shard_map/reduce_scatter | solution.py:57
  223.3 1.7 convert_element_type.7
  (9 shorter events, 0.1 us)
Async XLA Ops:
  6.5 134.7 %all-gather.2.cloned.1.call-start = ((), (), s32[]{:S(2)}) async-start(), calls=%async_computation.1 | async-start | bytes 15138816 | tf_op jit(solution)/shard_map/all_gather | solution.py:53
  10.8 212.5 %reduce-scatter.2.cloned.1.call-start = ((), (), s32[]{:S(2)}) async-start(), calls=%async_computation.2 | async-start | bytes 3538944 | tf_op jit(solution)/shard_map/reduce_scatter | solution.py:57
  18.0 10.5 %copy-start = (f32[768,8]{0,1:T(8,128)S(1)}, f32[768,8]{0,1:T(8,128)}, u32[]{:S(2)}) copy-start(f32[768,8]{0,1:T(8,128)} %param.6) | copy-start | bytes 73732
  18.0 10.5 %copy-start.1 = (s32[768,8]{0,1:T(8,128)S(1)}, s32[768,8]{0,1:T(8,128)}, u32[]{:S(2)}) copy-start(s32[768,8]{0,1:T(8,128)} %param.7) | copy-start | bytes 73732
Sparse Core Ops, SparseCore 0:
  10.9 130.2 all-gather.1
  179.3 43.9 reduce-scatter.1
where the time goes:
time: 234 us; the launch traced here: 232 us
  waiting for transfers between devices  157 us (67%)
  local copies, waits for them, and re-layouts  28.9 us (12%)
  matrix products  19.2 us (8%)
  between operations  13.5 us (6%)
  other arithmetic  13.4 us (6%)
    all_gather x1, waiting for transfers between devices, on_device(): lax.all_gather(serve_tiles(master_slots), 'rep', axis=0, tiled=True)  113 us
    reduce_scatter x1, waiting for transfers between devices, on_device(): lax.psum_scatter(gate_pick[:, None] * projection.reshape(lax.axis_size('e...  44.2 us
    dot_general x1, matrix products, on_device(): jnp.einsum('trk,rcfk->tcf', split_rows, placed, preferred_element_type=jn...  19.2 us
    gather x1, local copies, waits for them, and re-layouts, place_all(): return jnp.take(served_tiles, inverse, axis=0)  14.4 us
    unnamed x5, local copies, waits for them, and re-layouts  10.5 us
  transfers between devices with their start and end apart: 2, of which 2 were waited for; matrix products, arithmetic and copies ran while one was open for 8% of the time, Pallas kernels for 0%

commit v1 on v0

v1 whole, which is shorter than its diff:
```python
import functools

import jax
import jax.numpy as jnp
from jax import lax
from jax.experimental import pallas as pl
from jax.experimental.pallas import tpu as pltpu
from jax.sharding import PartitionSpec as P

D = 7168
FW = 1024
BLK = 128
SLOTS = 7
TOK = 768
ROWS = 96
PARTS = 8
PIECE = 2 * BLK // PARTS
OFFSETS = (0, 1, 3, 2)
PANELS = 8
CHUNKS = D // (BLK * PANELS)

QUANT_LIMIT = 448.0
GRID_STEP = 16.0
MESH = pl.DeviceIdType.MESH
NT = (((1,), (1,)), ((), ()))


def nearest_even(scaled):
    shifted = scaled * (1.0 / GRID_STEP) + 0.5
    level = jnp.floor(shifted)
    halfway = shifted == level
    odd_level = level - 2.0 * jnp.floor(level * 0.5) == 1.0
    level = jnp.where(jnp.logical_and(halfway, odd_level), level - 1.0, level)
    return level * GRID_STEP


def quantize(master_ref, peak_ref, recip_ref, pieces_ref):
    peak_ref[...] = jnp.zeros_like(peak_ref)
    for j in range(SLOTS):
        top = jnp.max(jnp.abs(master_ref[0, j]), axis=0, keepdims=True)
        for half in range(2):
            peak_ref[2 * j + half : 2 * j + half + 1, :] = top[:, half * BLK : (half + 1) * BLK]
    peak = jnp.broadcast_to(jnp.max(peak_ref[...], axis=1, keepdims=True), peak_ref.shape)
    scale = jnp.full_like(peak, 2.0**-30)
    recip = jnp.full_like(peak, 2.0**30)
    for exponent in range(-30, 1):
        exceeds = peak > QUANT_LIMIT * 2.0**exponent
        scale = jnp.where(exceeds, 2.0 ** (exponent + 1), scale)
        recip = jnp.where(exceeds, 2.0 ** (-exponent - 1), recip)
    peak_ref[...] = scale
    recip_ref[...] = recip
    for j in range(SLOTS):
        for half in range(2):
            r = 2 * j + half
            scaled = master_ref[0, j, :, half * BLK : (half + 1) * BLK] * recip_ref[r : r + 1, :]
            served = nearest_even(scaled) * peak_ref[r : r + 1, :]
            turned = served.T.astype(jnp.bfloat16)
            for q in range(PARTS // 2):
                pieces_ref[half * (PARTS // 2) + q, j] = turned[q * PIECE : (q + 1) * PIECE, :]


def slot_positions(owner):
    buckets = owner.shape[1]
    rows = lax.broadcasted_iota(jnp.int32, (buckets, buckets), 0)
    cols = lax.broadcasted_iota(jnp.int32, (buckets, buckets), 1)
    across = jnp.broadcast_to(owner, (buckets, buckets))
    down = jnp.sum(jnp.where(rows == cols, across, 0), axis=1, keepdims=True)
    earlier = jnp.logical_and(across == down, rows < cols)
    rank = jnp.sum(jnp.where(earlier, 1, 0), axis=0, keepdims=True)
    place = (owner & ~3) + ((owner & 1) << 1) + ((owner >> 1) & 1)
    return jnp.clip(place * SLOTS + rank, 0, buckets - 1)


def kernel(
    tokens_hbm, gates_ref, assign_ref, master_ref, owner_ref, out_ref,
    tok, w0, w1, w2, w3, pieces, peak, recip, line, lines, index, gate, partial, total, send_out, got_out,
    tok_sem, idx_sem,
    s_line, r_line, s_ex, r_ex, s_z, r_z, s_d, r_d, s_s, r_s, s_c, r_c, s_out, r_out,
):
    weights = (w0, w1, w2, w3)
    rep = lax.axis_index("rep")
    ex = lax.axis_index("exp")
    z, xh, c = rep // 4, (rep // 2) % 2, rep % 2
    xl, y = ex // 4, ex % 4
    half = (xl + xh) % 2
    part = half * 4 + y

    def dev(z_, xh_, c_, xl_, y_):
        return (z_ * 4 + xh_ * 2 + c_, xl_ * 4 + y_)

    up = dev((z + 1) % 8, xh, c, xl, y)
    down = dev((z + 7) % 8, xh, c, xl, y)
    side = dev(z, 1 - xh, c, 1 - xl, y)
    twin = dev(z, xh, 1 - c, xl, y)
    peers = [dev(z, xh, c, (xl + (n // 4)) % 2, (y + n) % 4) for n in range(1, 8)]

    barrier = pltpu.get_barrier_semaphore()
    for device in [up, down, side, twin] + peers:
        pl.semaphore_signal(barrier, inc=1, device_id=device, device_id_type=MESH)

    tok_copy = pltpu.make_async_copy(tokens_hbm, tok, tok_sem)
    tok_copy.start()
    quantize(master_ref, peak, recip, pieces)
    pl.semaphore_wait(barrier, 11)

    def send(src, dst, s_sem, r_sem, device):
        pltpu.make_async_remote_copy(
            src_ref=src, dst_ref=dst, send_sem=s_sem, recv_sem=r_sem, device_id=device, device_id_type=MESH
        ).start()

    def wait_slots(sem, n):
        ref = w0.at[0, pl.ds(0, n)]
        pltpu.make_async_copy(ref, ref, sem).wait()

    def base(z_):
        return ((z_ % 8) * 2 + c) * 14

    own = base(z) + 7 * xh
    at_s = 10 * xh
    at_d = 4 + 3 * xh
    at_d_side = 7 - 3 * xh
    at_ten = 4 * xh

    def sub(u):
        return (u + xh) % 2

    weights[0][xh, pl.ds(own, 7)] = pieces[part]
    for k in range(4):
        y_to = (y + 4 - OFFSETS[k]) % 4
        for j in range(2):
            if k == 0 and j == 1:
                continue
            xl_to = 1 - xl if k == 0 else (xl + j) % 2
            half_to = (xl_to + xh) % 2
            sub_to = (half_to + xl) % 2
            send(pieces.at[half_to * 4 + y_to], weights[k].at[sub_to, pl.ds(own, 7)], s_ex, r_ex.at[k],
                 dev(z, xh, c, xl_to, y_to))
        if k == 0:
            w = weights[0]
            send(w.at[xh, pl.ds(own, 7)], w.at[xh, pl.ds(own, 7)], s_z.at[0], r_z.at[0, 0], up)
            send(w.at[xh, pl.ds(own, 7)], w.at[xh, pl.ds(own, 7)], s_z.at[0], r_z.at[0, 0], down)
            ref = w.at[xh, pl.ds(base(z) + at_d, 3)]
            send(ref, ref, s_d.at[0], r_d.at[0], side)
            ref = w.at[xh, pl.ds(base(z) + at_s, 4)]
            send(ref, ref, s_s.at[0], r_s.at[0, 0], side)

    line[...] = jnp.zeros_like(line)
    line[:, 0:224] = slot_positions(owner_ref[...])
    lines[xh] = line[...]
    for k in range(4):
        y_to = (y + 4 - OFFSETS[k]) % 4
        for j in range(2):
            if k == 0 and j == 1:
                continue
            xl_to = 1 - xl if k == 0 else (xl + j) % 2
            sub_to = (xl_to + xh + xl) % 2
            send(line, lines.at[2 * k + sub_to], s_line, r_line, dev(z, xh, c, xl_to, y_to))

    def ring(u, lo, n, device, h):
        w = weights[u // 2]
        ref = w.at[sub(u), pl.ds(lo, n)]
        send(ref, ref, s_z.at[u], r_z.at[u, h], device)

    def over_side(u, z_, d):
        w = weights[u // 2]
        ref = w.at[sub(u), pl.ds(base(z_) + at_s, 4)]
        send(ref, ref, s_s.at[u], r_s.at[u, d], side)

    def exchange_d(k):
        if k == 0:
            return
        wait_slots(r_ex.at[k], 14)
        ref = weights[k].at[:, pl.ds(base(z) + at_d, 3)]
        send(ref, ref, s_d.at[2 * k], r_d.at[2 * k], side)

    def hop(u, h):
        if h == 1:
            if u >= 2:
                if u % 2 == 0:
                    wait_slots(r_d.at[u], 6)
                ring(u, base(z) + at_ten, 10, up, 0)
                ring(u, base(z) + at_ten, 10, down, 0)
                over_side(u, z, 0)
            elif u == 1:
                wait_slots(r_ex.at[0], 7)
                ring(1, own, 7, up, 0)
                ring(1, own, 7, down, 0)
                ref = weights[0].at[1 - xh, pl.ds(base(z) + at_d, 3)]
                send(ref, ref, s_d.at[1], r_d.at[1], side)
                over_side(1, z, 0)
                wait_slots(r_d.at[0], 3)
                ring(1, base(z) + at_d_side, 3, up, 0)
                ring(1, base(z) + at_d_side, 3, down, 0)
                wait_slots(r_d.at[1], 3)
                ring(0, base(z) + at_d_side, 3, up, 0)
                ring(0, base(z) + at_d_side, 3, down, 0)
            return
        d = h - 1
        if d <= 3:
            wait_slots(r_z.at[u, d - 1], 20)
            if h <= 3:
                ring(u, base(z + 8 - d) + at_ten, 10, up, d)
                ring(u, base(z + d) + at_ten, 10, down, d)
            else:
                ring(u, base(z + 8 - d) + 9 * xh, 5, up, d)
                ring(u, base(z + d) + 5 - xh, 5, down, d)
            over_side(u, z + 8 - d, d)
            over_side(u, z + d, d)
        else:
            wait_slots(r_z.at[u, 3], 10)
            over_side(u, z + 4, 4)

    def to_twin(k, d):
        n = 4 if d in (0, 4) else 8
        wait_slots(r_s.at[2 * k, d], n)
        wait_slots(r_s.at[2 * k + 1, d], n)
        for z_ in [z + d] if d in (0, 4) else [z + d, z + 8 - d]:
            ref = weights[k].at[:, pl.ds(base(z_), 14)]
            send(ref, ref, s_c.at[k], r_c.at[k], twin)

    def gates_of(u):
        e = ((half + u) % 2) * 4 + (y + OFFSETS[u // 2]) % 4
        pick = jnp.where(assign_ref[...] == e, gates_ref[...], 0.0)
        gate[u] = jnp.broadcast_to(jnp.sum(pick, axis=1, keepdims=True), (TOK, BLK))

    def chunks(k, lo, hi):
        w = weights[k]

        def body(ch, carry):
            tiles = []
            for i in range(PANELS):
                bucket = (ch * PANELS + i) * 4
                tiles.append(jnp.concatenate(
                    [w[s, index[2 * k + s, 0, bucket + g]] for s in range(2) for g in range(4)], axis=0))
            cols = pl.ds(pl.multiple_of(ch * (PANELS * BLK), PANELS * BLK), PANELS * BLK)
            partial[...] += lax.dot_general(
                tok[:, cols], jnp.concatenate(tiles, axis=1), NT, preferred_element_type=jnp.float32)
            return carry

        if lo == 0:
            wait_slots(r_c.at[k], 224)
            partial[...] = jnp.zeros_like(partial)
        lax.fori_loop(lo, hi, body, 0)
        if hi == CHUNKS:
            term = gate[2 * k] * partial[:, 0:BLK] + gate[2 * k + 1] * partial[:, BLK : 2 * BLK]
            total[...] = term if k == 0 else total[...] + term

    hop(1, 1)
    hop(0, 2)
    exchange_d(1)
    hop(1, 2)
    to_twin(0, 0)
    hop(0, 3)
    for u in range(4):
        gates_of(u)
    hop(2, 1)
    hop(0, 4)
    for u in range(4, 8):
        gates_of(u)
    wait_line = lines.at[pl.ds(0, 7)]
    pltpu.make_async_copy(wait_line, wait_line, r_line).wait()
    idx_copy = pltpu.make_async_copy(lines, index, idx_sem)
    idx_copy.start()
    idx_copy.wait()
    tok_copy.wait()

    work = [(k, lo, lo + 1) for k in range(4) for lo in range(CHUNKS)]
    ready = {0: 6, 1: 8, 2: 10, 3: 12}
    done = [0]

    def some_work(r, n):
        while n > 0 and done[0] < len(work) and r >= ready[work[done[0]][0]]:
            k, lo, hi = work[done[0]]
            m = 1
            while m < n and lo + m < CHUNKS:
                m += 1
            chunks(k, lo, lo + m)
            done[0] += m
            n -= m

    for r in range(3, 13):
        if r % 2 == 1 and (r + 1) // 2 < 4:
            exchange_d((r + 1) // 2)
        for h in range(6, 0, -1):
            u = r - (h - 1)
            if not 0 <= u < 8:
                continue
            if (r, h) == (3, 4):
                continue
            if h <= 5:
                hop(u, h)
            if u % 2 == 1 and h >= 2:
                to_twin(u // 2, h - 2)
            if h in (5, 3, 1):
                some_work(r, 2)
    some_work(99, 100)

    send_out[...] = total[...].astype(jnp.bfloat16)
    mine = pl.ds(pl.multiple_of(ex * ROWS, 16), ROWS)
    got_out[part] = send_out[mine, :]
    for n in range(1, 8):
        xl_to, y_to = (xl + n // 4) % 2, (y + n) % 4
        rows = pl.ds(pl.multiple_of((xl_to * 4 + y_to) * ROWS, 16), ROWS)
        send(send_out.at[rows], got_out.at[part], s_out, r_out, dev(z, xh, c, xl_to, y_to))

    wait_line = lines.at[pl.ds(0, 7)]
    pltpu.make_async_copy(wait_line, wait_line, s_line).wait()
    wait_slots(s_ex, 49)
    for u in range(8):
        wait_slots(s_z.at[u], 70)
        wait_slots(s_s.at[u], 32)
    wait_slots(s_d.at[0], 3)
    wait_slots(s_d.at[1], 3)
    for k in range(1, 4):
        wait_slots(s_d.at[2 * k], 6)
    for k in range(4):
        wait_slots(s_c.at[k], 224)
    seven = got_out.at[pl.ds(0, 7)]
    pltpu.make_async_copy(seven, seven, r_out).wait()
    pltpu.make_async_copy(seven, seven, s_out).wait()

    lanes = lax.broadcasted_iota(jnp.int32, (ROWS, BLK), 1) // PIECE
    for hh in range(2):
        got = [got_out[4 * hh + q].astype(jnp.float32) for q in range(4)]
        for g in range(4):
            tile = got[g]
            for q in range(4):
                if q != g:
                    tile = jnp.where(lanes == q, pltpu.roll(got[q], (q - g) * PIECE % BLK, 1), tile)
                else:
                    tile = jnp.where(lanes == q, got[q], tile)
            lo = g * 2 * BLK + hh * BLK
            out_ref[:, lo : lo + BLK] = tile.astype(jnp.bfloat16)


def on_device(tokens, gates, assign, master, owner):
    dma = pltpu.SemaphoreType.DMA
    vmem = pl.BlockSpec(memory_space=pltpu.VMEM)
    slots = master.shape[1] * lax.axis_size("rep")
    return pl.pallas_call(
        kernel,
        out_shape=jax.ShapeDtypeStruct((ROWS, FW), jnp.bfloat16),
        in_specs=[pl.BlockSpec(memory_space=pl.ANY), vmem, vmem, vmem, vmem],
        out_specs=vmem,
        scratch_shapes=[pltpu.VMEM((TOK, D), jnp.bfloat16)]
        + [pltpu.VMEM((2, slots, PIECE, BLK), jnp.bfloat16)] * 4
        + [
            pltpu.VMEM((PARTS, SLOTS, PIECE, BLK), jnp.bfloat16),
            pltpu.VMEM((16, BLK), jnp.float32),
            pltpu.VMEM((16, BLK), jnp.float32),
            pltpu.VMEM((1, 256), jnp.int32),
            pltpu.VMEM((8, 1, 256), jnp.int32),
            pltpu.SMEM((8, 1, 256), jnp.int32),
            pltpu.VMEM((8, TOK, BLK), jnp.float32),
            pltpu.VMEM((TOK, 2 * BLK), jnp.float32),
            pltpu.VMEM((TOK, BLK), jnp.float32),
            pltpu.VMEM((TOK, BLK), jnp.bfloat16),
            pltpu.VMEM((PARTS, ROWS, BLK), jnp.bfloat16),
            dma, dma,
            dma, dma,
            dma, dma((4,)),
            dma((8,)), dma((8, 4)),
            dma((8,)), dma((8,)),
            dma((8,)), dma((8, 5)),
            dma((4,)), dma((4,)),
            dma, dma,
        ],
        compiler_params=pltpu.CompilerParams(
            collective_id=0, has_side_effects=True, vmem_limit_bytes=52 * 1024 * 1024
        ),
        cost_estimate=pl.CostEstimate(
            flops=2 * TOK * D * FW, bytes_accessed=2 * TOK * D + 4 * SLOTS * BLK * 2 * BLK, transcendentals=0
        ),
        name="mixture",
    )(tokens, gates, assign, master, owner)


def solution(mesh):
    return jax.shard_map(
        on_device,
        mesh=mesh,
        in_specs=(
            P("rep", None),
            P("rep", None),
            P("rep", None),
            P("exp", "rep", None, None),
            P("exp", None),
        ),
        out_specs=P(("rep", "exp"), None),
        check_vma=False,
    )
```

time: 234 us -> 94.3 us (0.40)
  waiting for transfers between devices: 157 us -> 0 us
  Pallas kernels: 0 us -> 88.6 us
  local copies, waits for them, and re-layouts: 28.9 us -> 4.32 us
  matrix products: 19.2 us -> 0 us
  between operations: 13.5 us -> 0.03 us
  other arithmetic: 13.4 us -> 0 us
    all_gather x1 -> x0, waiting for transfers between devices: 113 us -> none  [on_device(): lax.all_gather(serve_tiles(master_slots), 'rep', axis=0, tiled=True)]
    pallas_call x0 -> x1, Pallas kernels: none -> 88.6 us  [on_device(): pl.pallas_call(kernel, out_shape=jax.ShapeDtypeStruct((ROWS, FW), jnp.bfl...]
    reduce_scatter x1 -> x0, waiting for transfers between devices: 44.2 us -> none  [on_device(): lax.psum_scatter(gate_pick[:, None] * projection.reshape(lax.axis_size('e...]
    dot_general x1 -> x0, matrix products: 19.2 us -> none  [on_device(): jnp.einsum('trk,rcfk->tcf', split_rows, placed, preferred_element_type=jn...]
    gather x1 -> x0, local copies, waits for them, and re-layouts: 14.4 us -> none  [place_all(): return jnp.take(served_tiles, inverse, axis=0)]
    sort x2 -> x0, other arithmetic: 7.01 us -> none  [the longest x1 3.84 us: on_device(): slot_bucket = jnp.argsort(owner[0], stable=True)]
    unnamed x5 -> x7, local copies, waits for them, and re-layouts: 10.5 us -> 4.32 us
    convert_element_type x2 -> x0, other arithmetic: 2.99 us -> none  [the longest x1 1.7 us: on_device(): return combined.astype(jnp.bfloat16)]
  transfers between devices with their start and end apart: 2 -> 0, of which waited for: 2 -> 0; matrix products, arithmetic and copies ran while one was open for 8% -> 0% of each run, Pallas kernels for 0% -> 0%
where the time goes in v1:
time: 94.3 us; the launch traced here: 93 us
  Pallas kernels  88.6 us (94%)
  local copies, waits for them, and re-layouts  4.32 us (5%)
    pallas_call x1, Pallas kernels, on_device(): pl.pallas_call(kernel, out_shape=jax.ShapeDtypeStruct((ROWS, FW), jnp.bfl...  88.6 us
    unnamed x7, local copies, waits for them, and re-layouts  4.32 us

profile of v1, /device:TPU:8, one launch (start us, length us, event | category | flops | bytes accessed | tf_op | source)
XLA Modules:
  0.0 93.0 jit_solution(18442699664483796874)
XLA Ops:
  0.0 0.9 copy.6.gates_ref
  0.9 0.9 copy.7.assign_ref
  1.8 0.0 copy-start
  1.8 1.2 %copy-done = f32[1,7,128,256]{3,2,1,0:T(8,128)S(1)} copy-done((f32[1,7,128,256]{3,2,1,0:T(8,128)S(1)}, f32[1,7,128,256]{3,2,1,0:T(8,128)}, u32[]{:S(2)}) %copy-start) | copy-done | bytes 917528
  3.0 0.0 copy-start.1
  3.0 0.7 copy-done.1
  3.7 88.6 %mixture.1 = bf16[96,1024]{1,0:T(8,128)(2,1)S(1)} custom-call(bf16[768,7168]{1,0:T(8,128)(2,1)} %tokens_hbm.1, f32[768,8]{1,0:T(8,128)S(1)} %copy.6.gates_ref, s32[768,8]{1,0:T(8,128)S(1)} %copy.7.assign_ref, f32[1,7,128,256]{3,2,1,0:T(8,128)S(1)} %copy-done, s32[1,224]{1,0:T(1,128)S(1)} %copy-done.1), custom_call_target="tpu_custom_call" | custom-call | flops 11274289152 | bytes 11927552 | tf_op jit(solution)/shard_map/mixture/pallas_call | solution.py:340
  92.3 0.7 copy.9
Async XLA Ops:
  1.8 1.2 %copy-start = (f32[1,7,128,256]{3,2,1,0:T(8,128)S(1)}, f32[1,7,128,256]{3,2,1,0:T(8,128)}, u32[]{:S(2)}) copy-start(f32[1,7,128,256]{3,2,1,0:T(8,128)} %master_ref.1) | copy-start | bytes 2752516
  3.0 0.7 copy-start.1

commit v2 on v1

v2 whole, which is shorter than its diff:
```python
import functools

import jax
import jax.numpy as jnp
from jax import lax
from jax.experimental import pallas as pl
from jax.experimental.pallas import tpu as pltpu
from jax.sharding import PartitionSpec as P

D = 7168
FW = 1024
BLK = 128
SLOTS = 7
TOK = 768
HALF = TOK // 2
ROWS = 96
PARTS = 8
PIECE = 2 * BLK // PARTS
OFFSETS = (0, 1, 3, 2)
DUAL = (2, 2, 2, 2, 3, 3, 3, 7)
PANELS = 8
CHUNKS = D // (BLK * PANELS)

QUANT_LIMIT = 448.0
GRID_STEP = 16.0
MESH = pl.DeviceIdType.MESH
NT = (((1,), (1,)), ((), ()))


ORDER = (
    ("own", 0, 0), ("own", 1, 0), ("dual", 1, 0), ("own", 2, 0), ("own", 3, 0), ("own", 4, 0), ("own", 5, 0),
    ("dual", 0, 0), ("twin", 0, 0), ("hop", 1, 2), ("dual", 2, 0), ("dual", 3, 0), ("twin", 1, 0), ("dual", 4, 0),
    ("own", 6, 0), ("dual", 5, 0), ("twin", 2, 0), ("own", 7, 0), ("hop", 0, 2), ("hop", 1, 3), ("hop", 2, 2),
    ("twin", 0, 1), ("hop", 3, 2), ("hop", 4, 2), ("hop", 0, 3), ("twin", 1, 1), ("hop", 1, 4), ("hop", 2, 3),
    ("hop", 3, 3), ("twin", 0, 2), ("hop", 4, 3), ("hop", 0, 4), ("hop", 1, 5), ("hop", 5, 2), ("twin", 1, 2),
    ("hop", 2, 4), ("hop", 3, 4), ("dual", 6, 0), ("dual", 7, 0), ("twin", 3, 0), ("twin", 0, 3), ("hop", 0, 5),
    ("hop", 4, 4), ("twin", 2, 1), ("hop", 5, 3), ("hop", 2, 5), ("hop", 3, 5), ("hop", 6, 2), ("twin", 1, 3),
    ("hop", 7, 2), ("twin", 0, 4), ("hop", 4, 5), ("hop", 5, 4), ("twin", 2, 2), ("work", 0, 1), ("hop", 6, 3),
    ("work", 0, 1), ("twin", 1, 4), ("work", 0, 1), ("twin", 3, 1), ("work", 0, 1), ("hop", 7, 3), ("work", 0, 1),
    ("hop", 5, 5), ("work", 0, 1), ("twin", 2, 3), ("work", 0, 1), ("hop", 6, 4), ("twin", 3, 2), ("work", 1, 1),
    ("work", 1, 1), ("work", 1, 1), ("twin", 2, 4), ("work", 1, 1), ("hop", 7, 4), ("work", 1, 1), ("hop", 6, 5),
    ("work", 1, 1), ("twin", 3, 3), ("work", 1, 1), ("work", 2, 1), ("work", 2, 1), ("work", 2, 1), ("hop", 7, 5),
    ("twin", 3, 4), ("work", 2, 1), ("work", 2, 1), ("work", 2, 1), ("work", 2, 1),
)


def nearest_even(scaled):
    shifted = scaled * (1.0 / GRID_STEP) + 0.5
    level = jnp.floor(shifted)
    halfway = shifted == level
    odd_level = level - 2.0 * jnp.floor(level * 0.5) == 1.0
    level = jnp.where(jnp.logical_and(halfway, odd_level), level - 1.0, level)
    return level * GRID_STEP


def quantize(master_ref, peak_ref, recip_ref, pieces_ref):
    peak_ref[...] = jnp.zeros_like(peak_ref)
    for j in range(SLOTS):
        top = jnp.max(jnp.abs(master_ref[0, j]), axis=0, keepdims=True)
        for half in range(2):
            peak_ref[2 * j + half : 2 * j + half + 1, :] = top[:, half * BLK : (half + 1) * BLK]
    peak = jnp.broadcast_to(jnp.max(peak_ref[...], axis=1, keepdims=True), peak_ref.shape)
    scale = jnp.full_like(peak, 2.0**-30)
    recip = jnp.full_like(peak, 2.0**30)
    for exponent in range(-30, 1):
        exceeds = peak > QUANT_LIMIT * 2.0**exponent
        scale = jnp.where(exceeds, 2.0 ** (exponent + 1), scale)
        recip = jnp.where(exceeds, 2.0 ** (-exponent - 1), recip)
    peak_ref[...] = scale
    recip_ref[...] = recip
    for j in range(SLOTS):
        for half in range(2):
            r = 2 * j + half
            scaled = master_ref[0, j, :, half * BLK : (half + 1) * BLK] * recip_ref[r : r + 1, :]
            served = nearest_even(scaled) * peak_ref[r : r + 1, :]
            turned = served.T.astype(jnp.bfloat16)
            for q in range(PARTS // 2):
                pieces_ref[half * (PARTS // 2) + q, j] = turned[q * PIECE : (q + 1) * PIECE, :]


def slot_positions(owner):
    buckets = owner.shape[1]
    rows = lax.broadcasted_iota(jnp.int32, (buckets, buckets), 0)
    cols = lax.broadcasted_iota(jnp.int32, (buckets, buckets), 1)
    across = jnp.broadcast_to(owner, (buckets, buckets))
    down = jnp.sum(jnp.where(rows == cols, across, 0), axis=1, keepdims=True)
    earlier = jnp.logical_and(across == down, rows < cols)
    rank = jnp.sum(jnp.where(earlier, 1, 0), axis=0, keepdims=True)
    place = (owner & ~3) + ((owner & 1) << 1) + ((owner >> 1) & 1)
    return jnp.clip(place * SLOTS + rank, 0, buckets - 1)


def kernel(
    tokens_hbm, gates_hbm, assign_hbm, master_hbm, owner_hbm, out_ref,
    gates_ref, assign_ref, master_ref, owner_ref, picks, tok, w0, w1, w2, w3, placed, pieces, peak, recip, line, lines, index, gate, partial, total, send_out, got_out,
    tok_sem, idx_sem, in_sem,
    s_line, r_line, s_ex, r_ex, s_z, r_z, s_d, r_d, s_s, r_s, s_c, r_c, s_out, r_out,
):
    weights = (w0, w1, w2, w3)
    rep = lax.axis_index("rep")
    ex = lax.axis_index("exp")
    z, xh, c = rep // 4, (rep // 2) % 2, rep % 2
    xl, y = ex // 4, ex % 4
    half = (xl + xh) % 2
    part = half * 4 + y

    def dev(z_, xh_, c_, xl_, y_):
        return (z_ * 4 + xh_ * 2 + c_, xl_ * 4 + y_)

    up = dev((z + 1) % 8, xh, c, xl, y)
    down = dev((z + 7) % 8, xh, c, xl, y)
    side = dev(z, 1 - xh, c, 1 - xl, y)
    twin = dev(z, xh, 1 - c, xl, y)
    peers = [dev(z, xh, c, (xl + (n // 4)) % 2, (y + n) % 4) for n in range(1, 8)]

    inputs = [
        pltpu.make_async_copy(src, dst, in_sem.at[n])
        for n, (src, dst) in enumerate(
            ((master_hbm, master_ref), (owner_hbm, owner_ref), (gates_hbm, gates_ref), (assign_hbm, assign_ref)))
    ]
    for copy in inputs:
        copy.start()
    barrier = pltpu.get_barrier_semaphore()
    for device in [up, down, side, twin] + peers:
        pl.semaphore_signal(barrier, inc=1, device_id=device, device_id_type=MESH)

    tok_copy = pltpu.make_async_copy(tokens_hbm, tok, tok_sem)
    tok_copy.start()
    for copy in inputs:
        copy.wait()
    quantize(master_ref, peak, recip, pieces)
    pl.semaphore_wait(barrier, 11)

    def send(src, dst, s_sem, r_sem, device):
        pltpu.make_async_remote_copy(
            src_ref=src, dst_ref=dst, send_sem=s_sem, recv_sem=r_sem, device_id=device, device_id_type=MESH
        ).start()

    def wait_slots(sem, n):
        ref = w0.at[0, pl.ds(0, n)]
        pltpu.make_async_copy(ref, ref, sem).wait()

    def base(z_):
        return ((z_ % 8) * 2 + c) * 14

    own = base(z) + 7 * xh

    def at_s(u):
        return (7 + DUAL[u]) * xh

    def at_d(u):
        return (7 - DUAL[u]) * (1 - xh) + 7 * xh

    def at_d_side(u):
        return 7 * (1 - xh) + (7 - DUAL[u]) * xh

    def at_both(u):
        return (7 - DUAL[u]) * xh

    def sub(u):
        return (u + xh) % 2 if u < 2 else u % 2

    weights[0][xh, pl.ds(own, 7)] = pieces[part]
    for k in range(4):
        y_to = (y + 4 - OFFSETS[k]) % 4
        for j in range(2):
            if k == 0 and j == 1:
                continue
            xl_to = 1 - xl if k == 0 else (xl + j) % 2
            half_to = (xl_to + xh) % 2
            sub_to = (half_to + xl) % 2
            send(pieces.at[half_to * 4 + y_to], weights[k].at[sub_to, pl.ds(own, 7)], s_ex, r_ex.at[k],
                 dev(z, xh, c, xl_to, y_to))

    def ring(u, lo, n, device, h):
        w = weights[u // 2]
        ref = w.at[sub(u), pl.ds(lo, n)]
        send(ref, ref, s_z.at[u], r_z.at[u, h], device)

    def over_side(u, z_, d):
        if DUAL[u] == 7:
            return
        w = weights[u // 2]
        ref = w.at[sub(u), pl.ds(base(z_) + at_s(u), 7 - DUAL[u])]
        send(ref, ref, s_s.at[u], r_s.at[u, d], side)

    def place_line():
        line[...] = jnp.zeros_like(line)
        line[:, 0:224] = slot_positions(owner_ref[...])
        lines[xh] = line[...]
        for k in range(4):
            y_to = (y + 4 - OFFSETS[k]) % 4
            for j in range(2):
                if k == 0 and j == 1:
                    continue
                xl_to = 1 - xl if k == 0 else (xl + j) % 2
                sub_to = (xl_to + xh + xl) % 2
                send(line, lines.at[2 * k + sub_to], s_line, r_line, dev(z, xh, c, xl_to, y_to))

    def own_slots(u):
        k = u // 2
        if u == 1:
            wait_slots(r_ex.at[0], 7)
        elif u >= 2 and u % 2 == 0:
            wait_slots(r_ex.at[k], 14)
        ring(u, own, 7, up, 0)
        ring(u, own, 7, down, 0)
        ref = weights[k].at[sub(u), pl.ds(base(z) + at_d(u), DUAL[u])]
        send(ref, ref, s_d.at[u], r_d.at[u], side)
        over_side(u, z, 0)

    def dual_slots(u):
        wait_slots(r_d.at[1 - u if u < 2 else u], DUAL[u])
        ring(u, base(z) + at_d_side(u), DUAL[u], up, 0)
        ring(u, base(z) + at_d_side(u), DUAL[u], down, 0)

    def hop(u, h):
        d = h - 1
        n = 7 + DUAL[u]
        if d <= 3:
            wait_slots(r_z.at[u, d - 1], 2 * n)
            if h <= 3:
                ring(u, base(z + 8 - d) + at_both(u), n, up, d)
                ring(u, base(z + d) + at_both(u), n, down, d)
            else:
                a = max((n + 1) // 2, 7 - DUAL[u])
                one, two, from_one, from_two = up, down, base(z + 8 - d), base(z + d)
                if u % 2 == 1:
                    one, two, from_one, from_two = two, one, from_two, from_one
                ring(u, from_one + (14 - a) * xh, a, one, d)
                ring(u, from_two + a * (1 - xh) + (7 - DUAL[u]) * xh, n - a, two, d)
            over_side(u, z + 8 - d, d)
            over_side(u, z + d, d)
        else:
            wait_slots(r_z.at[u, 3], n)
            over_side(u, z + 4, 4)

    def to_twin(k, d):
        for u in (2 * k, 2 * k + 1):
            if DUAL[u] < 7:
                wait_slots(r_s.at[u, d], (7 - DUAL[u]) * (1 if d in (0, 4) else 2))
        for z_ in [z + d] if d in (0, 4) else [z + d, z + 8 - d]:
            ref = weights[k].at[:, pl.ds(base(z_), 14)]
            send(ref, ref, s_c.at[k], r_c.at[k], twin)

    def pick_gates():
        for u in range(8):
            e = ((half + u) % 2) * 4 + (y + OFFSETS[u // 2]) % 4
            pick = jnp.where(assign_ref[...] == e, gates_ref[...], 0.0)
            picks[u : u + 1, :] = jnp.sum(pick, axis=0, keepdims=True)
        turned = picks[...].T
        for u in range(8):
            gate[u] = jnp.broadcast_to(turned[:, u : u + 1], (TOK, BLK))

    def fetch_index():
        every = lines.at[pl.ds(0, 7)]
        pltpu.make_async_copy(every, every, r_line).wait()
        idx_copy = pltpu.make_async_copy(lines, index, idx_sem)
        idx_copy.start()
        idx_copy.wait()
        tok_copy.wait()

    def tiles_of(k, ch):
        w = weights[k]
        tiles = []
        for i in range(PANELS):
            bucket = (ch * PANELS + i) * 4
            tiles.append(jnp.concatenate(
                [w[s, index[2 * k + s, 0, bucket + g]] for s in range(2) for g in range(4)], axis=0))
        return jnp.concatenate(tiles, axis=1)

    def columns(ch):
        return pl.ds(pl.multiple_of(ch * (PANELS * BLK), PANELS * BLK), PANELS * BLK)

    def chunks(k, lo, hi):
        def body(ch, carry):
            partial[...] += lax.dot_general(
                tok[:, columns(ch)], tiles_of(k, ch), NT, preferred_element_type=jnp.float32)
            return carry

        if lo == 0:
            wait_slots(r_c.at[k], 224)
            partial[...] = jnp.zeros_like(partial)
        lax.fori_loop(lo, hi, body, 0)
        if hi == CHUNKS:
            term = gate[2 * k] * partial[:, 0:BLK] + gate[2 * k + 1] * partial[:, BLK : 2 * BLK]
            total[...] = term if k == 0 else total[...] + term

    def last_chunks(far):
        rows = pl.ds(pl.multiple_of(((xl + 1) % 2 if far else xl) * HALF, HALF), HALF)
        acc = partial.at[pl.ds(0, HALF)]

        def body(ch, carry):
            tiles = tiles_of(3, ch)
            placed[:, columns(ch)] = tiles
            acc[...] += lax.dot_general(
                tok[rows, columns(ch)], tiles, NT, preferred_element_type=jnp.float32)
            return carry

        if far:
            acc[...] = jnp.zeros_like(acc)
            lax.fori_loop(0, CHUNKS, body, 0)
        else:
            acc[...] = lax.dot_general(tok[rows, :], placed[...], NT, preferred_element_type=jnp.float32)
        term = gate[6, rows, :] * acc[:, 0:BLK] + gate[7, rows, :] * acc[:, BLK : 2 * BLK]
        send_out[rows, :] = (total[rows, :] + term).astype(jnp.bfloat16)
        for n in (2, 1, 3, 0):
            xl_to, y_to = (xl + 1) % 2 if far else xl, (y + n) % 4
            to = pl.ds(pl.multiple_of((xl_to * 4 + y_to) * ROWS, 16), ROWS)
            if far or n > 0:
                send(send_out.at[to], got_out.at[part], s_out, r_out, dev(z, xh, c, xl_to, y_to))
            else:
                got_out[part] = send_out[to, :]

    at = 0
    chunk = 0
    while at < len(ORDER):
        kind, u, h = ORDER[at]
        if kind == "own":
            own_slots(u)
            if u == 0:
                place_line()
        elif kind == "dual":
            dual_slots(u)
        elif kind == "hop":
            hop(u, h)
        elif kind == "twin":
            to_twin(u, h)
        else:
            n = 1
            while at + n < len(ORDER) and ORDER[at + n][:2] == ("work", u):
                n += 1
            if u == 0 and chunk == 0:
                fetch_index()
            chunks(u, chunk, chunk + n)
            chunk = (chunk + n) % CHUNKS
            at += n - 1
        if at == 8:
            pick_gates()
        at += 1

    wait_slots(r_c.at[3], 224)
    last_chunks(True)
    last_chunks(False)

    every = lines.at[pl.ds(0, 7)]
    pltpu.make_async_copy(every, every, s_line).wait()
    wait_slots(s_ex, 49)
    for u in range(8):
        wait_slots(s_z.at[u], 7 * (7 + DUAL[u]))
        wait_slots(s_d.at[u], DUAL[u])
        if DUAL[u] < 7:
            wait_slots(s_s.at[u], 8 * (7 - DUAL[u]))
    for k in range(4):
        wait_slots(s_c.at[k], 224)
    seven = got_out.at[pl.ds(0, 7)]
    pltpu.make_async_copy(seven, seven, r_out).wait()
    pltpu.make_async_copy(seven, seven, s_out).wait()

    lanes = lax.broadcasted_iota(jnp.int32, (ROWS, BLK), 1) // PIECE
    for hh in range(2):
        got = [got_out[4 * hh + q].astype(jnp.float32) for q in range(4)]
        for g in range(4):
            tile = got[g]
            for q in range(4):
                if q != g:
                    tile = jnp.where(lanes == q, pltpu.roll(got[q], (q - g) * PIECE % BLK, 1), tile)
                else:
                    tile = jnp.where(lanes == q, got[q], tile)
            lo = g * 2 * BLK + hh * BLK
            out_ref[:, lo : lo + BLK] = tile.astype(jnp.bfloat16)


def on_device(tokens, gates, assign, master, owner):
    dma = pltpu.SemaphoreType.DMA
    vmem = pl.BlockSpec(memory_space=pltpu.VMEM)
    slots = master.shape[1] * lax.axis_size("rep")
    return pl.pallas_call(
        kernel,
        out_shape=jax.ShapeDtypeStruct((ROWS, FW), jnp.bfloat16),
        in_specs=[pl.BlockSpec(memory_space=pltpu.HBM)] * 5,
        out_specs=vmem,
        scratch_shapes=[
            pltpu.VMEM((8, TOK), jnp.float32),
            pltpu.VMEM((8, TOK), jnp.int32),
            pltpu.VMEM(master.shape, jnp.float32),
            pltpu.VMEM(owner.shape, jnp.int32),
            pltpu.VMEM((8, TOK), jnp.float32),
            pltpu.VMEM((TOK, D), jnp.bfloat16),
        ]
        + [pltpu.VMEM((2, slots, PIECE, BLK), jnp.bfloat16)] * 4
        + [
            pltpu.VMEM((2 * BLK, D), jnp.bfloat16),
            pltpu.VMEM((PARTS, SLOTS, PIECE, BLK), jnp.bfloat16),
            pltpu.VMEM((16, BLK), jnp.float32),
            pltpu.VMEM((16, BLK), jnp.float32),
            pltpu.VMEM((1, 256), jnp.int32),
            pltpu.VMEM((8, 1, 256), jnp.int32),
            pltpu.SMEM((8, 1, 256), jnp.int32),
            pltpu.VMEM((8, TOK, BLK), jnp.float32),
            pltpu.VMEM((TOK, 2 * BLK), jnp.float32),
            pltpu.VMEM((TOK, BLK), jnp.float32),
            pltpu.VMEM((TOK, BLK), jnp.bfloat16),
            pltpu.VMEM((PARTS, ROWS, BLK), jnp.bfloat16),
            dma, dma, dma((4,)),
            dma, dma,
            dma, dma((4,)),
            dma((8,)), dma((8, 4)),
            dma((8,)), dma((8,)),
            dma((8,)), dma((8, 5)),
            dma((4,)), dma((4,)),
            dma, dma,
        ],
        compiler_params=pltpu.CompilerParams(
            collective_id=0, has_side_effects=True, vmem_limit_bytes=54 * 1024 * 1024
        ),
        cost_estimate=pl.CostEstimate(
            flops=2 * TOK * D * FW, bytes_accessed=2 * TOK * D + 4 * SLOTS * BLK * 2 * BLK, transcendentals=0
        ),
        name="mixture",
    )(tokens, gates.T, assign.T, master, owner)


def solution(mesh):
    return jax.shard_map(
        on_device,
        mesh=mesh,
        in_specs=(
            P("rep", None),
            P("rep", None),
            P("rep", None),
            P("exp", "rep", None, None),
            P("exp", None),
        ),
        out_specs=P(("rep", "exp"), None),
        check_vma=False,
    )
```

time: 94.3 us -> 84.1 us (0.89); the launches traced: 93 us -> 83.8 us
  Pallas kernels: 88.6 us -> 82.2 us
  local copies, waits for them, and re-layouts: 4.32 us -> 1.62 us
    pallas_call x1, Pallas kernels: 88.6 us -> 82.2 us  [on_device(): pl.pallas_call(kernel, out_shape=jax.ShapeDtypeStruct((ROWS, FW), jnp.bfl...]
    unnamed x7 -> x1, local copies, waits for them, and re-layouts: 4.32 us -> 1.62 us
where the time goes in v2:
time: 84.1 us; the launch traced here: 83.8 us
  Pallas kernels  82.2 us (98%)
  local copies, waits for them, and re-layouts  1.62 us (2%)
    pallas_call x1, Pallas kernels, on_device(): pl.pallas_call(kernel, out_shape=jax.ShapeDtypeStruct((ROWS, FW), jnp.bfl...  82.2 us

profile of v2, /device:TPU:8, one launch (start us, length us, event | category | flops | bytes accessed | tf_op | source)
XLA Modules:
  0.0 83.8 jit_solution(771796455156768517)
XLA Ops:
  0.0 82.2 %mixture.1 = bf16[96,1024]{1,0:T(8,128)(2,1)} custom-call(bf16[768,7168]{1,0:T(8,128)(2,1)} %tokens_hbm.1, f32[8,768]{1,0:T(8,128)} %bitcast.2, s32[8,768]{1,0:T(8,128)} %bitcast.3, f32[1,7,128,256]{3,2,1,0:T(8,128)} %master_hbm.1, s32[1,224]{1,0:T(1,128)} %owner_hbm.1), custom_call_target="tpu_custom_call" | custom-call | flops 11274289152 | bytes 11927552 | tf_op jit(solution)/shard_map/mixture/pallas_call | solution.py:378
  82.2 1.6 %copy.7 = bf16[96,1024]{1,0:T(8,128)(2,1)} copy(bf16[96,1024]{1,0:T(8,128)(2,1)} %mixture.1) | data formatting | bytes 393216

commit v3 on v2

--- a/solution.py
+++ b/solution.py
@@ -17,7 +17,7 @@
 PARTS = 8
 PIECE = 2 * BLK // PARTS
 OFFSETS = (0, 1, 3, 2)
-DUAL = (2, 2, 2, 2, 3, 3, 3, 7)
+DUAL = (2, 2, 2, 2, 2, 2, 7, 7)
 PANELS = 8
 CHUNKS = D // (BLK * PANELS)
 
@@ -28,19 +28,19 @@
 
 
 ORDER = (
-    ("own", 0, 0), ("own", 1, 0), ("dual", 1, 0), ("own", 2, 0), ("own", 3, 0), ("own", 4, 0), ("own", 5, 0),
-    ("dual", 0, 0), ("twin", 0, 0), ("hop", 1, 2), ("dual", 2, 0), ("dual", 3, 0), ("twin", 1, 0), ("dual", 4, 0),
-    ("own", 6, 0), ("dual", 5, 0), ("twin", 2, 0), ("own", 7, 0), ("hop", 0, 2), ("hop", 1, 3), ("hop", 2, 2),
-    ("twin", 0, 1), ("hop", 3, 2), ("hop", 4, 2), ("hop", 0, 3), ("twin", 1, 1), ("hop", 1, 4), ("hop", 2, 3),
-    ("hop", 3, 3), ("twin", 0, 2), ("hop", 4, 3), ("hop", 0, 4), ("hop", 1, 5), ("hop", 5, 2), ("twin", 1, 2),
-    ("hop", 2, 4), ("hop", 3, 4), ("dual", 6, 0), ("dual", 7, 0), ("twin", 3, 0), ("twin", 0, 3), ("hop", 0, 5),
-    ("hop", 4, 4), ("twin", 2, 1), ("hop", 5, 3), ("hop", 2, 5), ("hop", 3, 5), ("hop", 6, 2), ("twin", 1, 3),
-    ("hop", 7, 2), ("twin", 0, 4), ("hop", 4, 5), ("hop", 5, 4), ("twin", 2, 2), ("work", 0, 1), ("hop", 6, 3),
-    ("work", 0, 1), ("twin", 1, 4), ("work", 0, 1), ("twin", 3, 1), ("work", 0, 1), ("hop", 7, 3), ("work", 0, 1),
-    ("hop", 5, 5), ("work", 0, 1), ("twin", 2, 3), ("work", 0, 1), ("hop", 6, 4), ("twin", 3, 2), ("work", 1, 1),
-    ("work", 1, 1), ("work", 1, 1), ("twin", 2, 4), ("work", 1, 1), ("hop", 7, 4), ("work", 1, 1), ("hop", 6, 5),
-    ("work", 1, 1), ("twin", 3, 3), ("work", 1, 1), ("work", 2, 1), ("work", 2, 1), ("work", 2, 1), ("hop", 7, 5),
-    ("twin", 3, 4), ("work", 2, 1), ("work", 2, 1), ("work", 2, 1), ("work", 2, 1),
+    ("own", 0, 0), ("own", 1, 0), ("own", 2, 0), ("dual", 1, 0), ("own", 3, 0), ("own", 4, 0), ("dual", 0, 0),
+    ("own", 5, 0), ("dual", 2, 0), ("hop", 1, 2), ("own", 6, 0), ("dual", 3, 0), ("hop", 0, 2), ("hop", 2, 2),
+    ("hop", 1, 3), ("own", 7, 0), ("dual", 5, 0), ("hop", 3, 2), ("twin", 1, 0), ("hop", 0, 3), ("hop", 2, 3),
+    ("dual", 4, 0), ("hop", 1, 4), ("hop", 3, 3), ("hop", 0, 4), ("hop", 5, 2), ("twin", 2, 0), ("dual", 6, 0),
+    ("hop", 1, 5), ("hop", 2, 4), ("twin", 0, 2), ("twin", 0, 1), ("hop", 0, 5), ("hop", 3, 4), ("hop", 4, 2),
+    ("hop", 5, 3), ("dual", 7, 0), ("twin", 0, 3), ("hop", 3, 5), ("twin", 0, 0), ("twin", 1, 1), ("hop", 2, 5),
+    ("hop", 4, 3), ("twin", 0, 4), ("hop", 5, 4), ("hop", 6, 2), ("hop", 4, 4), ("twin", 1, 2), ("hop", 7, 2),
+    ("work", 0, 1), ("hop", 5, 5), ("work", 0, 1), ("twin", 1, 3), ("work", 0, 1), ("twin", 1, 4), ("twin", 3, 0),
+    ("work", 0, 1), ("hop", 6, 3), ("twin", 2, 1), ("hop", 4, 5), ("twin", 3, 1), ("work", 0, 1), ("work", 0, 1),
+    ("twin", 2, 2), ("work", 0, 1), ("hop", 7, 3), ("work", 1, 1), ("work", 1, 1), ("twin", 2, 3), ("work", 1, 1),
+    ("work", 1, 1), ("twin", 2, 4), ("hop", 6, 4), ("work", 1, 1), ("work", 1, 1), ("work", 1, 1), ("hop", 7, 4),
+    ("twin", 3, 3), ("twin", 3, 2), ("work", 2, 1), ("work", 2, 1), ("hop", 6, 5), ("twin", 3, 4), ("work", 2, 1),
+    ("work", 2, 1), ("work", 2, 1), ("hop", 7, 5), ("work", 2, 1), ("work", 2, 1),
 )
 
 
@@ -111,6 +111,8 @@
     down = dev((z + 7) % 8, xh, c, xl, y)
     side = dev(z, 1 - xh, c, 1 - xl, y)
     twin = dev(z, xh, 1 - c, xl, y)
+    up_twin = dev((z + 1) % 8, xh, 1 - c, xl, y)
+    down_twin = dev((z + 7) % 8, xh, 1 - c, xl, y)
     peers = [dev(z, xh, c, (xl + (n // 4)) % 2, (y + n) % 4) for n in range(1, 8)]
 
     inputs = [
@@ -121,7 +123,7 @@
     for copy in inputs:
         copy.start()
     barrier = pltpu.get_barrier_semaphore()
-    for device in [up, down, side, twin] + peers:
+    for device in [up, down, side, twin, up_twin, down_twin] + peers:
         pl.semaphore_signal(barrier, inc=1, device_id=device, device_id_type=MESH)
 
     tok_copy = pltpu.make_async_copy(tokens_hbm, tok, tok_sem)
@@ -129,7 +131,7 @@
     for copy in inputs:
         copy.wait()
     quantize(master_ref, peak, recip, pieces)
-    pl.semaphore_wait(barrier, 11)
+    pl.semaphore_wait(barrier, 13)
 
     def send(src, dst, s_sem, r_sem, device):
         pltpu.make_async_remote_copy(
@@ -229,6 +231,13 @@
                     one, two, from_one, from_two = two, one, from_two, from_one
                 ring(u, from_one + (14 - a) * xh, a, one, d)
                 ring(u, from_two + a * (1 - xh) + (7 - DUAL[u]) * xh, n - a, two, d)
+                if u == 7:
+                    for lo, m, device in (
+                        (from_one + (14 - a) * xh, a, (down_twin)),
+                        (from_two + a * (1 - xh) + (7 - DUAL[u]) * xh, n - a, (up_twin)),
+                    ):
+                        ref = weights[3].at[1, pl.ds(lo, m)]
+                        send(ref, ref, s_c.at[3], r_c.at[3], device)
             over_side(u, z + 8 - d, d)
             over_side(u, z + d, d)
         else:
@@ -236,11 +245,12 @@
             over_side(u, z + 4, 4)
 
     def to_twin(k, d):
+        last = (k, d) == (3, 4)
         for u in (2 * k, 2 * k + 1):
             if DUAL[u] < 7:
                 wait_slots(r_s.at[u, d], (7 - DUAL[u]) * (1 if d in (0, 4) else 2))
         for z_ in [z + d] if d in (0, 4) else [z + d, z + 8 - d]:
-            ref = weights[k].at[:, pl.ds(base(z_), 14)]
+            ref = weights[k].at[pl.ds(0, 1 if last else 2), pl.ds(base(z_), 14)]
             send(ref, ref, s_c.at[k], r_c.at[k], twin)
 
     def pick_gates():
@@ -252,13 +262,12 @@
         for u in range(8):
             gate[u] = jnp.broadcast_to(turned[:, u : u + 1], (TOK, BLK))
 
+    idx_copy = pltpu.make_async_copy(lines, index, idx_sem)
+
     def fetch_index():
         every = lines.at[pl.ds(0, 7)]
         pltpu.make_async_copy(every, every, r_line).wait()
-        idx_copy = pltpu.make_async_copy(lines, index, idx_sem)
         idx_copy.start()
-        idx_copy.wait()
-        tok_copy.wait()
 
     def tiles_of(k, ch):
         w = weights[k]
@@ -272,19 +281,36 @@
     def columns(ch):
         return pl.ds(pl.multiple_of(ch * (PANELS * BLK), PANELS * BLK), PANELS * BLK)
 
-    def chunks(k, lo, hi):
+    def step(kind, u, h):
+        if kind == "own":
+            own_slots(u)
+            if u == 0:
+                place_line()
+        elif kind == "dual":
+            dual_slots(u)
+        elif kind == "hop":
+            hop(u, h)
+        else:
+            to_twin(u, h)
+
+    def chunks(k, between, fresh):
+        wait_slots(r_c.at[k], 224)
+        partial[...] = jnp.zeros_like(partial)
+
         def body(ch, carry):
             partial[...] += lax.dot_general(
                 tok[:, columns(ch)], tiles_of(k, ch), NT, preferred_element_type=jnp.float32)
+            for n, steps in enumerate(between):
+                if steps:
+                    @pl.when(ch == n)
+                    def _():
+                        for each in steps:
+                            step(*each)
             return carry
 
-        if lo == 0:
-            wait_slots(r_c.at[k], 224)
-            partial[...] = jnp.zeros_like(partial)
-        lax.fori_loop(lo, hi, body, 0)
-        if hi == CHUNKS:
-            term = gate[2 * k] * partial[:, 0:BLK] + gate[2 * k + 1] * partial[:, BLK : 2 * BLK]
-            total[...] = term if k == 0 else total[...] + term
+        lax.fori_loop(0, CHUNKS, body, 0)
+        term = gate[2 * k] * partial[:, 0:BLK] + gate[2 * k + 1] * partial[:, BLK : 2 * BLK]
+        total[...] = term if fresh else total[...] + term
 
     def last_chunks(far):
         rows = pl.ds(pl.multiple_of(((xl + 1) % 2 if far else xl) * HALF, HALF), HALF)
@@ -312,32 +338,19 @@
             else:
                 got_out[part] = send_out[to, :]
 
-    at = 0
-    chunk = 0
-    while at < len(ORDER):
-        kind, u, h = ORDER[at]
-        if kind == "own":
-            own_slots(u)
-            if u == 0:
-                place_line()
-        elif kind == "dual":
-            dual_slots(u)
-        elif kind == "hop":
-            hop(u, h)
-        elif kind == "twin":
-            to_twin(u, h)
-        else:
-            n = 1
-            while at + n < len(ORDER) and ORDER[at + n][:2] == ("work", u):
-                n += 1
-            if u == 0 and chunk == 0:
-                fetch_index()
-            chunks(u, chunk, chunk + n)
-            chunk = (chunk + n) % CHUNKS
-            at += n - 1
-        if at == 8:
+    first = [n for n, each in enumerate(ORDER) if each[0] == "work"]
+    for n, each in enumerate(ORDER[: first[0]]):
+        step(*each)
+        if n == 8:
             pick_gates()
-        at += 1
+        elif n == 14:
+            fetch_index()
+    idx_copy.wait()
+    tok_copy.wait()
+    ends = first[1:] + [len(ORDER)]
+    for n in range(0, 3 * CHUNKS, CHUNKS):
+        between = [ORDER[lo + 1 : hi] for lo, hi in zip(first[n : n + CHUNKS], ends[n:])]
+        chunks(ORDER[first[n]][1], between, n == 0)
 
     wait_slots(r_c.at[3], 224)
     last_chunks(True)

time: 84.1 us -> 80.3 us (0.955)
  Pallas kernels: 82.2 us -> 78.6 us
    pallas_call x1, Pallas kernels: 82.2 us -> 78.6 us  [on_device(): pl.pallas_call(kernel, out_shape=jax.ShapeDtypeStruct((ROWS, FW), jnp.bfl...]
where the time goes in v3:
time: 80.3 us; the launch traced here: 80.2 us
  Pallas kernels  78.6 us (98%)
  local copies, waits for them, and re-layouts  1.62 us (2%)
    pallas_call x1, Pallas kernels, on_device(): pl.pallas_call(kernel, out_shape=jax.ShapeDtypeStruct((ROWS, FW), jnp.bfl...  78.6 us
    unnamed x1, local copies, waits for them, and re-layouts  1.62 us

profile of v3, /device:TPU:8, one launch (start us, length us, event | category | flops | bytes accessed | tf_op | source)
XLA Modules:
  0.0 80.2 jit_solution(13273400637244047216)
XLA Ops:
  0.0 78.6 %mixture.1 = bf16[96,1024]{1,0:T(8,128)(2,1)} custom-call(bf16[768,7168]{1,0:T(8,128)(2,1)} %tokens_hbm.1, f32[8,768]{1,0:T(8,128)} %bitcast.2, s32[8,768]{1,0:T(8,128)} %bitcast.3, f32[1,7,128,256]{3,2,1,0:T(8,128)} %master_hbm.1, s32[1,224]{1,0:T(1,128)} %owner_hbm.1), custom_call_target="tpu_custom_call" | custom-call | flops 11274289152 | bytes 11927552 | tf_op jit(solution)/shard_map/mixture/pallas_call | solution.py:391
  78.6 1.6 %copy.7 = bf16[96,1024]{1,0:T(8,128)(2,1)} copy(bf16[96,1024]{1,0:T(8,128)(2,1)} %mixture.1) | data formatting | bytes 393216

commit v4 on v3

--- a/solution.py
+++ b/solution.py
@@ -19,6 +19,7 @@
 OFFSETS = (0, 1, 3, 2)
 DUAL = (2, 2, 2, 2, 2, 2, 7, 7)
 PANELS = 8
+LAST_PANELS = 14
 CHUNKS = D // (BLK * PANELS)
 
 QUANT_LIMIT = 448.0
@@ -269,17 +270,17 @@
         pltpu.make_async_copy(every, every, r_line).wait()
         idx_copy.start()
 
-    def tiles_of(k, ch):
+    def tiles_of(k, ch, panels=PANELS):
         w = weights[k]
         tiles = []
-        for i in range(PANELS):
-            bucket = (ch * PANELS + i) * 4
+        for i in range(panels):
+            bucket = (ch * panels + i) * 4
             tiles.append(jnp.concatenate(
                 [w[s, index[2 * k + s, 0, bucket + g]] for s in range(2) for g in range(4)], axis=0))
         return jnp.concatenate(tiles, axis=1)
 
-    def columns(ch):
-        return pl.ds(pl.multiple_of(ch * (PANELS * BLK), PANELS * BLK), PANELS * BLK)
+    def columns(ch, panels=PANELS):
+        return pl.ds(pl.multiple_of(ch * (panels * BLK), panels * BLK), panels * BLK)
 
     def step(kind, u, h):
         if kind == "own":
@@ -317,15 +318,15 @@
         acc = partial.at[pl.ds(0, HALF)]
 
         def body(ch, carry):
-            tiles = tiles_of(3, ch)
-            placed[:, columns(ch)] = tiles
+            tiles = tiles_of(3, ch, LAST_PANELS)
+            placed[:, columns(ch, LAST_PANELS)] = tiles
             acc[...] += lax.dot_general(
-                tok[rows, columns(ch)], tiles, NT, preferred_element_type=jnp.float32)
+                tok[rows, columns(ch, LAST_PANELS)], tiles, NT, preferred_element_type=jnp.float32)
             return carry
 
         if far:
             acc[...] = jnp.zeros_like(acc)
-            lax.fori_loop(0, CHUNKS, body, 0)
+            lax.fori_loop(0, D // (LAST_PANELS * BLK), body, 0)
         else:
             acc[...] = lax.dot_general(tok[rows, :], placed[...], NT, preferred_element_type=jnp.float32)
         term = gate[6, rows, :] * acc[:, 0:BLK] + gate[7, rows, :] * acc[:, BLK : 2 * BLK]

time: 80.3 us -> 79.7 us (level)
  no operation moved by 1% of the time
where the time goes in v4:
time: 79.7 us; the launch traced here: 79.6 us
  Pallas kernels  77.9 us (98%)
  local copies, waits for them, and re-layouts  1.62 us (2%)
    pallas_call x1, Pallas kernels, on_device(): pl.pallas_call(kernel, out_shape=jax.ShapeDtypeStruct((ROWS, FW), jnp.bfl...  77.9 us
    unnamed x1, local copies, waits for them, and re-layouts  1.62 us

profile of v4, /device:TPU:8, one launch (start us, length us, event | category | flops | bytes accessed | tf_op | source)
XLA Modules:
  0.0 79.6 jit_solution(14179678857212412162)
XLA Ops:
  0.0 77.9 %mixture.1 = bf16[96,1024]{1,0:T(8,128)(2,1)} custom-call(bf16[768,7168]{1,0:T(8,128)(2,1)} %tokens_hbm.1, f32[8,768]{1,0:T(8,128)} %bitcast.2, s32[8,768]{1,0:T(8,128)} %bitcast.3, f32[1,7,128,256]{3,2,1,0:T(8,128)} %master_hbm.1, s32[1,224]{1,0:T(1,128)} %owner_hbm.1), custom_call_target="tpu_custom_call" | custom-call | flops 11274289152 | bytes 11927552 | tf_op jit(solution)/shard_map/mixture/pallas_call | solution.py:392
  78.0 1.6 %copy.7 = bf16[96,1024]{1,0:T(8,128)(2,1)} copy(bf16[96,1024]{1,0:T(8,128)(2,1)} %mixture.1) | data formatting | bytes 393216
